TPU v7x, 32 devices: a whole 2x2x4 slice. The times are simulated.
32 devices in a mesh: groups: 2 (over x), expert: 8 (over z, y), cuts: 2 (over core).
Axes of the slice: x: 2, y: 2, z: 4, core: 2. Of those that a mesh axis runs over, the one named last changes fastest.
Arguments:
- tokens: bfloat16 [64, 2, 6144], P(('groups', 'expert', 'cuts')), parts along dimension 0, may hold values from -6 to 6
- routes: int32 [64, 2, 2], P(('groups', 'expert', 'cuts')), parts along dimension 0, may hold values from 0 to 7, all different within a row
- gates: float32 [64, 2, 2], P(('groups', 'expert', 'cuts')), parts along dimension 0, may hold values from 0.1 to 0.9
- ranking: int32 [16], P('groups'), parts along dimension 0, may hold values from 0 to 7, each once
- counts: int32 [2, 32], P(None, ('groups', 'expert', 'cuts')), parts along dimension 1, may hold values from 1 to 2, 24 in all within a row
- w_gate: bfloat16 [2, 6144, 8192], P(None, None, ('expert', 'cuts')), may hold values from -0.078125 to 0.078125
- w_up: bfloat16 [2, 6144, 8192], P(None, None, ('expert', 'cuts')), may hold values from -0.078125 to 0.078125
- w_down: bfloat16 [2, 8192, 6144], P(None, ('expert', 'cuts')), may hold values from -0.0625 to 0.0625
Outputs:
- expert_out: bfloat16 [64, 2, 6144], P(('groups', 'expert', 'cuts')), parts along dimension 0
There are 2 independent parts, one for each index of `groups`. A program takes and returns all parts, laid end to end along the dimension named above; an argument that names none is the same for every part. Nothing has to cross between parts.
All inputs are finite; a program needn't handle non-finite values. No bound on the sum of `counts` on one device may be relied on, other than what follows from the above.
Results may differ from a plain program's by a relative error of at most 0.0067.
Values may be sent and summed in bfloat16 or wider, within the bound.
A program may use at most 128 MiB of HBM per device.

v0:
```python
import jax
import jax.numpy as jnp
from jax import lax
from jax.sharding import PartitionSpec as P

HOT = 2


def expert_terms(rows, weights, w_gate, w_up, w_down):
    gate = jnp.einsum("rsd,hdc->rshc", rows, w_gate, preferred_element_type=jnp.float32)
    upper = jnp.einsum("rsd,hdc->rshc", rows, w_up, preferred_element_type=jnp.float32)
    hidden = (jax.nn.silu(gate) * upper * weights[:, :, :, None].astype(jnp.float32)).astype(
        jnp.bfloat16
    )
    return jnp.einsum("rshc,hcd->rsd", hidden, w_down, preferred_element_type=jnp.float32)


def run_block(inputs, weights, w_gate, w_up, w_down):
    gathered, gathered_weights = (
        lax.all_gather(inputs, ("expert", "cuts"), axis=0, tiled=True),
        lax.all_gather(weights, ("expert", "cuts"), axis=0, tiled=True),
    )
    summed = lax.psum_scatter(
        expert_terms(gathered, gathered_weights, w_gate, w_up, w_down),
        ("expert", "cuts"),
        scatter_dimension=0,
        tiled=True,
    )
    return summed.astype(jnp.bfloat16)


def on_device(tokens, routes, gates, ranking, counts, w_gate, w_up, w_down):
    hot = ranking[:HOT]
    match = (routes[:, :, :, None] == hot[None, None, None, :]).astype(jnp.float32)
    weight = jnp.sum(gates[:, :, :, None] * match, axis=2)
    slots = lax.broadcasted_iota(jnp.int32, (tokens.shape[0], tokens.shape[1]), 0)
    live = (slots < counts[:, 0][None, :]).astype(jnp.float32)
    weight = (weight * live[:, :, None]).astype(jnp.bfloat16)
    return run_block(tokens, weight, w_gate, w_up, w_down)


def solution(mesh):
    in_specs = (
        P(("groups", "expert", "cuts"), None, None),
        P(("groups", "expert", "cuts"), None, None),
        P(("groups", "expert", "cuts"), None, None),
        P("groups"),
        P(None, ("groups", "expert", "cuts")),
        P(None, None, ("expert", "cuts")),
        P(None, None, ("expert", "cuts")),
        P(None, ("expert", "cuts"), None),
    )
    out_specs = P(("groups", "expert", "cuts"), None, None)
    return jax.shard_map(
        on_device, mesh=mesh, in_specs=in_specs, out_specs=out_specs, check_vma=False
    )
```

profile of v0, /device:TPU:0, one launch (start us, length us, event | category | flops | bytes accessed | tf_op | source)
XLA Modules:
  0.0 137.1 jit_solution(11383634740327483612)
XLA Ops:
  0.0 0.0 copy-start.2
  0.0 0.0 copy-start
  0.0 0.0 copy-start.1
  0.0 0.0 copy-start.3
  0.0 25.9 %all_gather.6 = bf16[32,2,6144]{2,1,0:T(2,128)(2,1)S(1)} all-gather(bf16[2,2,6144]{2,1,0:T(2,128)(2,1)} %param.8), channel_id=1, replica_groups=mesh['groups'=2,'expert'=8,'cuts'=2] {'expert','cuts'}, dimensions={0}, use_global_device_ids=true | all-gather | bytes 835584 | tf_op jit(solution)/shard_map/all_gather | solution.py:20
  25.9 6.9 %fusion.4 = f32[32,2,2,512]{3,0,2,1:T(8,128)S(1)} fusion(bf16[2,6144,512]{2,1,0:T(8,128)(2,1)} %param.13, bf16[32,2,6144,1]{2,1,0,3:T(2,128)(2,1)S(1)} %bitcast.27), kind=kOutput, calls=%fused_computation.4 | convolution fusion | flops 805306368 | bytes 13631488 | tf_op jit(solution)/shard_map/rsd,hdc->rshc/dot_general | solution.py:10
  32.8 0.0 copy-done.2
  32.8 0.0 copy-done
  32.8 0.0 copy-done.1
  32.8 0.1 fusion.30
  32.9 0.0 copy-done.3
  32.9 0.1 multiply_convert_fusion
  33.0 17.4 %all_gather.7 = bf16[32,2,2]{2,1,0:T(2,128)(2,1)S(1)} all-gather(bf16[2,2,2]{2,1,0:T(2,128)(2,1)S(1)} %multiply_convert_fusion), channel_id=1, replica_groups=mesh['groups'=2,'expert'=8,'cuts'=2] {'expert','cuts'}, dimensions={0}, use_global_device_ids=true | all-gather | bytes 272 | tf_op jit(solution)/shard_map/all_gather | solution.py:21
  50.4 0.1 copy.20
  50.5 0.0 copy-start.4
  50.5 12.7 %fusion.6 = f32[32,2,6144]{2,0,1:T(8,128)S(1)} fusion(bf16[2,512,6144]{2,1,0:T(8,128)(2,1)} %param.15, bf16[2,6144,512]{2,1,0:T(8,128)(2,1)} %param.14, bf16[32,2,6144,1]{2,1,0,3:T(2,128)(2,1)S(1)} %bitcast.28, f32[32,2,2,512]{3,0,2,1:T(8,128)S(1)} %fusion.4, f32[32,2,2]{0,2,1:T(2,128)S(1)} %convert_element_type.23), kind=kOutput, calls=%fused_computation.6 | convolution fusion | flops 1611071488 | bytes 27787776 | tf_op jit(solution)/shard_map/rshc,hcd->rsd/dot_general | solution.py:15
  63.3 71.8 %all-reduce.2 = bf16[32,2,6144]{2,0,1:T(8,128)(2,1)S(1)} all-reduce(f32[32,2,6144]{2,0,1:T(8,128)S(1)} %fusion.6), channel_id=2, replica_groups=mesh['groups'=2,'expert'=8,'cuts'=2] {'expert','cuts'}, use_global_device_ids=true, to_apply=%region_1.2.clone | all-reduce | flops 393216 | bytes 2359296
  135.1 0.0 copy-done.4
  135.1 0.6 dynamic-slice
  136.4 0.1 dynamic-slice_convert_fusion
  136.4 0.7 copy.21
  (2 shorter events, 0.0 us)
Async XLA Ops:
  0.0 32.8 %copy-start.2 = (s32[8]{0:T(128)S(1)}, s32[8]{0:T(128)}, u32[]{:S(2)}) copy-start(s32[8]{0:T(128)} %param.11) | copy-start | bytes 100
  0.0 32.8 %copy-start = (f32[2,2,2]{2,1,0:T(2,128)S(1)}, f32[2,2,2]{2,1,0:T(2,128)}, u32[]{:S(2)}) copy-start(f32[2,2,2]{2,1,0:T(2,128)} %param.10) | copy-start | bytes 100
  0.0 32.8 %copy-start.1 = (s32[2,2,2]{2,1,0:T(2,128)S(1)}, s32[2,2,2]{2,1,0:T(2,128)}, u32[]{:S(2)}) copy-start(s32[2,2,2]{2,1,0:T(2,128)} %param.9) | copy-start | bytes 100
  0.0 32.9 %copy-start.3 = (s32[2,1]{0,1:T(1,128)S(1)}, s32[2,1]{0,1:T(1,128)}, u32[]{:S(2)}) copy-start(s32[2,1]{0,1:T(1,128)} %param.12) | copy-start | bytes 28
  50.5 84.6 %copy-start.4 = (u32[32]{0:T(128)S(1)}, u32[32]{0:T(128)}, u32[]{:S(2)}) copy-start(u32[32]{0:T(128)} %constant.12) | copy-start | bytes 388
where the time goes:
time: 137 us
  blocking collectives  115 us (84%)
  matrix products  19.6 us (14%)
  local copies, waits for them, and re-layouts  1.42 us (1%)
    unnamed x1, blocking collectives  71.8 us
    all_gather x1, blocking collectives, run_block(): lax.all_gather(inputs, ('expert', 'cuts'), axis=0, tiled=True)  25.9 us
    all_gather x1, blocking collectives, run_block(): lax.all_gather(weights, ('expert', 'cuts'), axis=0, tiled=True)  17.4 us
    dot_general x1, matrix products, expert_terms(): jnp.einsum('rshc,hcd->rsd', hidden, w_down, preferred_element_type=jnp.fl...  12.7 us
    dot_general x1, matrix products, expert_terms(): jnp.einsum('rsd,hdc->rshc', rows, w_gate, preferred_element_type=jnp.floa...  6.92 us

commit v1 on v0

v1 whole, which is shorter than its diff:
```python
import functools

import jax
import jax.numpy as jnp
from jax import lax
from jax.experimental import pallas as pl
from jax.experimental.pallas import tpu as pltpu
from jax.sharding import PartitionSpec as P

HOT = 2
LANES = 128
K_PARTS = 4
COL_PARTS = 6
MESH = pl.DeviceIdType.MESH


def kernel(
    planes, tokens, routes, gates, ranking, counts, w_gate, w_up, w_down, out,
    gathered, rows_f32, rows, gate_w, up_w, down_w, g_acc, u_acc, hidden,
    send_a, recv_a, send_b, recv_b, send_c, recv_c, total,
    token_sem, gate_sems, up_sems, down_sems,
    gz_send, gz_recv, gy_send, gy_recv, gc_send, gc_recv,
    a_send, a_recv, b_send, b_recv, c_send, c_recv,
):
    own_rows, steps, width = tokens.shape
    block = own_rows * steps
    part = planes * block
    depth = width // K_PARTS
    cols = width // COL_PARTS
    group = lax.axis_index("groups")
    expert = lax.axis_index("expert")
    c = lax.axis_index("cuts")
    z = expert // 2
    y = expert % 2

    def device(zz, yy, cc):
        return (group, zz * 2 + yy, cc)

    def slot(zz, yy, cc):
        return pl.ds(((zz * 2 + yy) * 2 + cc) * own_rows, own_rows)

    def plane(dz):
        return lax.rem(z + dz, planes)

    mine = slot(z, y, c)
    token_copy = pltpu.make_async_copy(
        tokens, gathered.at[mine, :, pl.ds(0, width)], token_sem
    )
    token_copy.start()
    gate_copies, up_copies, down_copies = [], [], []
    for h in range(HOT):
        for k in range(K_PARTS):
            at = pl.ds(k * depth, depth)
            i = h * K_PARTS + k
            gate_copies.append(
                pltpu.make_async_copy(w_gate.at[h, at, :], gate_w.at[h, at, :], gate_sems.at[i])
            )
            up_copies.append(
                pltpu.make_async_copy(w_up.at[h, at, :], up_w.at[h, at, :], up_sems.at[i])
            )
            gate_copies[-1].start()
            up_copies[-1].start()
    for j in range(COL_PARTS):
        at = pl.ds(j * cols, cols)
        down_copies.append(
            pltpu.make_async_copy(w_down.at[:, :, at], down_w.at[j], down_sems.at[j])
        )
        down_copies[-1].start()

    barrier = pltpu.get_barrier_semaphore()
    for dz in range(1, planes):
        pl.semaphore_signal(barrier, inc=1, device_id=device(plane(dz), y, c), device_id_type=MESH)
    pl.semaphore_signal(barrier, inc=1, device_id=device(z, 1 - y, c), device_id_type=MESH)
    pl.semaphore_signal(barrier, inc=1, device_id=device(z, y, 1 - c), device_id_type=MESH)

    lane = lax.broadcasted_iota(jnp.int32, (1, LANES), 1)
    for r in range(own_rows):
        lines = []
        for s in range(steps):
            line = jnp.zeros((1, LANES), jnp.float32)
            for h in range(HOT):
                value = jnp.float32(0)
                for k in range(routes.shape[2]):
                    value = value + jnp.where(routes[r, s, k] == ranking[h], gates[r, s, k], 0.0)
                value = jnp.where(r < counts[s, 0], value, 0.0)
                line = jnp.where(lane == h, value, line)
            lines.append(line)
        own = ((z * 2 + y) * 2 + c) * own_rows + r
        gathered[own, :, pl.ds(width, LANES)] = jnp.concatenate(lines, axis=0).astype(jnp.bfloat16)
    token_copy.wait()
    pl.semaphore_wait(barrier, planes + 1)

    def remote(src, dst, send, recv, target):
        return pltpu.make_async_remote_copy(
            src_ref=src, dst_ref=dst, send_sem=send, recv_sem=recv,
            device_id=target, device_id_type=MESH,
        )

    def share(where, send, recv, target):
        return remote(gathered.at[where], gathered.at[where], send, recv, target)

    to_y, to_c = device(z, 1 - y, c), device(z, y, 1 - c)
    z_copies = [
        share(mine, gz_send.at[dz], gz_recv.at[dz], device(plane(dz), y, c))
        for dz in range(1, planes)
    ]
    y_copies = [
        share(slot(plane(planes - dz), y, c), gy_send.at[dz], gy_recv.at[dz], to_y)
        for dz in range(planes)
    ]
    c_copies = [
        [
            share(
                slot(plane(planes - dz), yy, c),
                gc_send.at[i * planes + dz], gc_recv.at[i * planes + dz], to_c,
            )
            for dz in range(planes)
        ]
        for i, yy in enumerate((y, 1 - y))
    ]
    for copy in z_copies:
        copy.start()
    y_copies[0].start()
    c_copies[0][0].start()
    for dz in range(1, planes):
        z_copies[dz - 1].wait_recv()
        y_copies[dz].start()
        c_copies[0][dz].start()
    for dz in range(planes):
        y_copies[dz].wait_recv()
        c_copies[1][dz].start()
    for i in range(2):
        for copy in c_copies[i]:
            copy.wait_recv()

    for dc in range(2):
        for dy in range(2):
            for dz in range(planes):
                cc = 1 - c if dc == 0 else c
                yy = 1 - y if dy == 0 else y
                first = ((plane(dz) * 2 + yy) * 2 + cc) * own_rows
                base = ((dc * 2 + dy) * planes + dz) * block
                for r in range(own_rows):
                    rows_f32[base + r * steps:base + (r + 1) * steps, :] = gathered[
                        first + r
                    ].astype(jnp.float32)
    rows[...] = rows_f32[:, :width].astype(jnp.bfloat16)

    for h in range(HOT):
        for k in range(K_PARTS):
            i = h * K_PARTS + k
            at = slice(k * depth, (k + 1) * depth)
            gate_copies[i].wait()
            g = jnp.dot(rows[:, at], gate_w[h, at, :], preferred_element_type=jnp.float32)
            up_copies[i].wait()
            u = jnp.dot(rows[:, at], up_w[h, at, :], preferred_element_type=jnp.float32)
            if k == 0:
                g_acc[...] = g
                u_acc[...] = u
            else:
                g_acc[...] += g
                u_acc[...] += u
        g = g_acc[...]
        weight = rows_f32[:, width + h:width + h + 1]
        hidden[h] = (g / (1.0 + jnp.exp(-g)) * u_acc[...] * weight).astype(jnp.bfloat16)

    a_copies = [
        remote(send_a.at[j], recv_a.at[j], a_send.at[j], a_recv.at[j], to_c)
        for j in range(COL_PARTS)
    ]
    b_copies = [
        remote(send_b.at[j], recv_b.at[j], b_send.at[j], b_recv.at[j], to_y)
        for j in range(COL_PARTS)
    ]
    d_copies = [
        [
            remote(
                send_c.at[j, dz], recv_c.at[j, dz],
                c_send.at[j * planes + dz], c_recv.at[j * planes + dz],
                device(plane(dz), y, c),
            )
            for dz in range(1, planes)
        ]
        for j in range(COL_PARTS)
    ]

    def down(j):
        down_copies[j].wait()
        p = jnp.dot(hidden[0], down_w[j, 0], preferred_element_type=jnp.float32)
        p = p + jnp.dot(hidden[1], down_w[j, 1], preferred_element_type=jnp.float32)
        send_a[j] = p[:2 * part].astype(jnp.bfloat16)
        a_copies[j].start()
        total[j] = p[2 * part:]

    def after_a(j):
        a_copies[j].wait_recv()
        send_b[j] = (total[j, :part] + recv_a[j, :part].astype(jnp.float32)).astype(jnp.bfloat16)
        b_copies[j].start()
        total[j, part:] += recv_a[j, part:].astype(jnp.float32)

    def after_b(j):
        b_copies[j].wait_recv()
        total[j, part:] += recv_b[j].astype(jnp.float32)
        for dz in range(1, planes):
            base = part + dz * block
            send_c[j, dz] = total[j, base:base + block].astype(jnp.bfloat16)
            d_copies[j][dz - 1].start()

    def after_c(j):
        result = total[j, part:part + block]
        for dz in range(1, planes):
            d_copies[j][dz - 1].wait_recv()
            result = result + recv_c[j, dz].astype(jnp.float32)
        for r in range(own_rows):
            out[r, :, j * cols:(j + 1) * cols] = result[r * steps:(r + 1) * steps].astype(jnp.bfloat16)

    for j in range(COL_PARTS + 3):
        if j < COL_PARTS:
            down(j)
        if 0 <= j - 1 < COL_PARTS:
            after_a(j - 1)
        if 0 <= j - 2 < COL_PARTS:
            after_b(j - 2)
    for j in range(COL_PARTS):
        after_c(j)

    for copy in z_copies + y_copies + c_copies[0] + c_copies[1] + a_copies + b_copies:
        copy.wait_send()
    for copies in d_copies:
        for copy in copies:
            copy.wait_send()


def on_device(devices, tokens, routes, gates, ranking, counts, w_gate, w_up, w_down):
    own_rows, steps, width = tokens.shape
    planes = devices // 4
    block = own_rows * steps
    part = planes * block
    units = w_gate.shape[2]
    cols = width // COL_PARTS
    bf16, f32 = jnp.bfloat16, jnp.float32
    dma = pltpu.SemaphoreType.DMA
    in_vmem = pl.BlockSpec(memory_space=pltpu.VMEM)
    in_smem = pl.BlockSpec(memory_space=pltpu.SMEM)
    anywhere = pl.BlockSpec(memory_space=pl.ANY)
    return pl.pallas_call(
        functools.partial(kernel, planes),
        out_shape=jax.ShapeDtypeStruct(tokens.shape, bf16),
        in_specs=[anywhere] + [in_smem] * 4 + [anywhere] * 3,
        out_specs=in_vmem,
        scratch_shapes=[
            pltpu.VMEM((devices * own_rows, steps, width + LANES), bf16),
            pltpu.VMEM((4 * part, width + LANES), f32),
            pltpu.VMEM((4 * part, width), bf16),
            pltpu.VMEM((HOT, width, units), bf16),
            pltpu.VMEM((HOT, width, units), bf16),
            pltpu.VMEM((COL_PARTS, HOT, units, cols), bf16),
            pltpu.VMEM((4 * part, units), f32),
            pltpu.VMEM((4 * part, units), f32),
            pltpu.VMEM((HOT, 4 * part, units), bf16),
            pltpu.VMEM((COL_PARTS, 2 * part, cols), bf16),
            pltpu.VMEM((COL_PARTS, 2 * part, cols), bf16),
            pltpu.VMEM((COL_PARTS, part, cols), bf16),
            pltpu.VMEM((COL_PARTS, part, cols), bf16),
            pltpu.VMEM((COL_PARTS, planes, block, cols), bf16),
            pltpu.VMEM((COL_PARTS, planes, block, cols), bf16),
            pltpu.VMEM((COL_PARTS, 2 * part, cols), f32),
            dma,
            dma((HOT * K_PARTS,)),
            dma((HOT * K_PARTS,)),
            dma((COL_PARTS,)),
            dma((planes,)), dma((planes,)),
            dma((planes,)), dma((planes,)),
            dma((2 * planes,)), dma((2 * planes,)),
            dma((COL_PARTS,)), dma((COL_PARTS,)),
            dma((COL_PARTS,)), dma((COL_PARTS,)),
            dma((COL_PARTS * planes,)), dma((COL_PARTS * planes,)),
        ],
        compiler_params=pltpu.CompilerParams(
            collective_id=0, has_side_effects=True, vmem_limit_bytes=60 << 20
        ),
    )(tokens, routes, gates, ranking, counts, w_gate, w_up, w_down)


def solution(mesh):
    rows = ("groups", "expert", "cuts")
    units = ("expert", "cuts")
    in_specs = (
        P(rows, None, None),
        P(rows, None, None),
        P(rows, None, None),
        P("groups"),
        P(None, rows),
        P(None, None, units),
        P(None, None, units),
        P(None, units, None),
    )
    devices = mesh.shape["expert"] * mesh.shape["cuts"]
    return jax.shard_map(
        functools.partial(on_device, devices), mesh=mesh, in_specs=in_specs,
        out_specs=P(rows, None, None), check_vma=False,
    )
```

time: 137 us -> 50.7 us (0.37)
  blocking collectives: 115 us -> 0 us
  Pallas kernels: 0 us -> 47.7 us
  matrix products: 19.6 us -> 0 us
    unnamed x1 -> x0, blocking collectives: 71.8 us -> none
    pallas_call x0 -> x1, Pallas kernels: none -> 47.7 us  [on_device(): pl.pallas_call(functools.partial(kernel, planes), out_shape=jax.ShapeDtyp...]
    all_gather x2 -> x0, blocking collectives: 43.3 us -> none  [the longest x1 25.9 us: run_block(): lax.all_gather(inputs, ('expert', 'cuts'), axis=0, tiled=True)]
    dot_general x2 -> x0, matrix products: 19.6 us -> none  [the longest x1 12.7 us: expert_terms(): jnp.einsum('rshc,hcd->rsd', hidden, w_down, preferred_element_type=jnp.fl...]
    unnamed x11 -> x2, local copies, waits for them, and re-layouts: 0.6 us -> 2.75 us
where the time goes in v1:
time: 50.7 us; the launch traced here: 50.5 us
  Pallas kernels  47.7 us (94%)
  local copies, waits for them, and re-layouts  2.75 us (5%)
    pallas_call x1, Pallas kernels, on_device(): pl.pallas_call(functools.partial(kernel, planes), out_shape=jax.ShapeDtyp...  47.7 us
    unnamed x2, local copies, waits for them, and re-layouts  2.75 us

profile of v1, /device:TPU:0, one launch (start us, length us, event | category | flops | bytes accessed | tf_op | source)
XLA Modules:
  0.0 50.5 jit_solution(11029369318690006956)
XLA Ops:
  0.0 1.3 %copy.9.counts = s32[2,1]{1,0:T(2,128)} copy(s32[2,1]{0,1:T(1,128)} %param.12) | data formatting | bytes 16 | tf_op args[4]
  1.3 47.7 %shard_map.82 = bf16[2,2,6144]{2,1,0:T(2,128)(2,1)} custom-call(bf16[2,2,6144]{2,1,0:T(2,128)(2,1)} %tokens.1, s32[2,2,2]{2,1,0:T(2,128)} %routes.1, f32[2,2,2]{2,1,0:T(2,128)} %gates.1, s32[8]{0:T(128)} %ranking.1, s32[2,1]{1,0:T(2,128)} %copy.9.counts, bf16[2,6144,512]{2,1,0:T(8,128)(2,1)} %w_gate.1, bf16[2,6144,512]{2,1,0:T(8,128)(2,1)} %w_up.1, ...), custom_call_target="tpu_custom_call" | custom-call | tf_op jit(solution)/shard_map/pallas_call | solution.py:246
  49.1 1.5 %copy.11 = bf16[2,2,6144]{2,1,0:T(2,128)(2,1)} copy(bf16[2,2,6144]{2,1,0:T(2,128)(2,1)} %shard_map.82) | data formatting | bytes 98304

commit v2 on v1

--- a/solution.py
+++ b/solution.py
@@ -11,11 +11,15 @@
 LANES = 128
 K_PARTS = 4
 COL_PARTS = 6
+FIRST = 6
+STEP = 3
+LAG = 3
 MESH = pl.DeviceIdType.MESH
 
 
 def kernel(
-    planes, tokens, routes, gates, ranking, counts, w_gate, w_up, w_down, out,
+    planes, tokens, routes_hbm, gates_hbm, ranking_hbm, counts_hbm, w_gate, w_up, w_down, out,
+    routes, gates, ranking, counts, own_tokens, own_block, small_sems,
     gathered, rows_f32, rows, gate_w, up_w, down_w, g_acc, u_acc, hidden,
     send_a, recv_a, send_b, recv_b, send_c, recv_c, total,
     token_sem, gate_sems, up_sems, down_sems,
@@ -37,17 +41,28 @@
         return (group, zz * 2 + yy, cc)
 
     def slot(zz, yy, cc):
-        return pl.ds(((zz * 2 + yy) * 2 + cc) * own_rows, own_rows)
+        return (zz * 2 + yy) * 2 + cc
 
     def plane(dz):
         return lax.rem(z + dz, planes)
 
-    mine = slot(z, y, c)
-    token_copy = pltpu.make_async_copy(
-        tokens, gathered.at[mine, :, pl.ds(0, width)], token_sem
-    )
+    to_y, to_c = device(z, 1 - y, c), device(z, y, 1 - c)
+    barrier = pltpu.get_barrier_semaphore()
+    for target in [device(plane(dz), y, c) for dz in range(1, planes)] + [to_y, to_c]:
+        pl.semaphore_signal(barrier, inc=1, device_id=target, device_id_type=MESH)
+
+    small_copies = [
+        pltpu.make_async_copy(src, dst, small_sems.at[i])
+        for i, (src, dst) in enumerate((
+            (routes_hbm, routes), (gates_hbm, gates), (ranking_hbm, ranking), (counts_hbm, counts)
+        ))
+    ]
+    token_copy = pltpu.make_async_copy(tokens, own_tokens, token_sem)
     token_copy.start()
-    gate_copies, up_copies, down_copies = [], [], []
+    for copy in small_copies:
+        copy.start()
+
+    gate_copies, up_copies, down_copies, waiting = [], [], [], []
     for h in range(HOT):
         for k in range(K_PARTS):
             at = pl.ds(k * depth, depth)
@@ -58,36 +73,39 @@
             up_copies.append(
                 pltpu.make_async_copy(w_up.at[h, at, :], up_w.at[h, at, :], up_sems.at[i])
             )
-            gate_copies[-1].start()
-            up_copies[-1].start()
+            waiting += [gate_copies[-1], up_copies[-1]]
     for j in range(COL_PARTS):
         at = pl.ds(j * cols, cols)
         down_copies.append(
             pltpu.make_async_copy(w_down.at[:, :, at], down_w.at[j], down_sems.at[j])
         )
-        down_copies[-1].start()
-
-    barrier = pltpu.get_barrier_semaphore()
-    for dz in range(1, planes):
-        pl.semaphore_signal(barrier, inc=1, device_id=device(plane(dz), y, c), device_id_type=MESH)
-    pl.semaphore_signal(barrier, inc=1, device_id=device(z, 1 - y, c), device_id_type=MESH)
-    pl.semaphore_signal(barrier, inc=1, device_id=device(z, y, 1 - c), device_id_type=MESH)
-
+    waiting += down_copies
+
+    def stream(count):
+        for copy in waiting[:count]:
+            copy.start()
+        del waiting[:count]
+
+    stream(FIRST)
+    for copy in small_copies:
+        copy.wait()
+
+    mine = slot(z, y, c)
     lane = lax.broadcasted_iota(jnp.int32, (1, LANES), 1)
     for r in range(own_rows):
-        lines = []
         for s in range(steps):
             line = jnp.zeros((1, LANES), jnp.float32)
             for h in range(HOT):
                 value = jnp.float32(0)
                 for k in range(routes.shape[2]):
                     value = value + jnp.where(routes[r, s, k] == ranking[h], gates[r, s, k], 0.0)
-                value = jnp.where(r < counts[s, 0], value, 0.0)
+                value = jnp.where(r < counts[s], value, 0.0)
                 line = jnp.where(lane == h, value, line)
-            lines.append(line)
-        own = ((z * 2 + y) * 2 + c) * own_rows + r
-        gathered[own, :, pl.ds(width, LANES)] = jnp.concatenate(lines, axis=0).astype(jnp.bfloat16)
+            own_block[r * steps + s:r * steps + s + 1, width:] = line
     token_copy.wait()
+    for r in range(own_rows):
+        own_block[r * steps:(r + 1) * steps, :width] = own_tokens[r].astype(jnp.float32)
+    gathered[mine] = own_block[...].astype(jnp.bfloat16)
     pl.semaphore_wait(barrier, planes + 1)
 
     def remote(src, dst, send, recv, target):
@@ -99,7 +117,6 @@
     def share(where, send, recv, target):
         return remote(gathered.at[where], gathered.at[where], send, recv, target)
 
-    to_y, to_c = device(z, 1 - y, c), device(z, y, 1 - c)
     z_copies = [
         share(mine, gz_send.at[dz], gz_recv.at[dz], device(plane(dz), y, c))
         for dz in range(1, planes)
@@ -118,32 +135,37 @@
         ]
         for i, yy in enumerate((y, 1 - y))
     ]
+
+    def keep(dc, dy, back):
+        dz = (planes - back) % planes
+        base = ((dc * 2 + dy) * planes + dz) * block
+        source = slot(plane(dz), y if dy else 1 - y, c if dc else 1 - c)
+        rows_f32[base:base + block, :] = gathered[source].astype(jnp.float32)
+
     for copy in z_copies:
         copy.start()
     y_copies[0].start()
     c_copies[0][0].start()
-    for dz in range(1, planes):
-        z_copies[dz - 1].wait_recv()
-        y_copies[dz].start()
-        c_copies[0][dz].start()
-    for dz in range(planes):
-        y_copies[dz].wait_recv()
-        c_copies[1][dz].start()
-    for i in range(2):
-        for copy in c_copies[i]:
-            copy.wait_recv()
-
-    for dc in range(2):
-        for dy in range(2):
-            for dz in range(planes):
-                cc = 1 - c if dc == 0 else c
-                yy = 1 - y if dy == 0 else y
-                first = ((plane(dz) * 2 + yy) * 2 + cc) * own_rows
-                base = ((dc * 2 + dy) * planes + dz) * block
-                for r in range(own_rows):
-                    rows_f32[base + r * steps:base + (r + 1) * steps, :] = gathered[
-                        first + r
-                    ].astype(jnp.float32)
+    stream(STEP)
+    keep(1, 1, 0)
+    for back in range(1, planes + 1):
+        if back < planes:
+            z_copies[back - 1].wait_recv()
+            y_copies[back].start()
+            c_copies[0][back].start()
+            stream(STEP)
+            keep(1, 1, back)
+        y_copies[back - 1].wait_recv()
+        c_copies[1][back - 1].start()
+        stream(STEP)
+        keep(1, 0, back - 1)
+    stream(len(waiting))
+    for back in range(planes):
+        c_copies[0][back].wait_recv()
+        keep(0, 1, back)
+    for back in range(planes):
+        c_copies[1][back].wait_recv()
+        keep(0, 0, back)
     rows[...] = rows_f32[:, :width].astype(jnp.bfloat16)
 
     for h in range(HOT):
@@ -214,13 +236,13 @@
         for r in range(own_rows):
             out[r, :, j * cols:(j + 1) * cols] = result[r * steps:(r + 1) * steps].astype(jnp.bfloat16)
 
-    for j in range(COL_PARTS + 3):
+    for j in range(COL_PARTS + 2 * LAG):
         if j < COL_PARTS:
             down(j)
-        if 0 <= j - 1 < COL_PARTS:
-            after_a(j - 1)
-        if 0 <= j - 2 < COL_PARTS:
-            after_b(j - 2)
+        if 0 <= j - LAG < COL_PARTS:
+            after_a(j - LAG)
+        if 0 <= j - 2 * LAG < COL_PARTS:
+            after_b(j - 2 * LAG)
     for j in range(COL_PARTS):
         after_c(j)
 
@@ -232,6 +254,7 @@
 
 
 def on_device(devices, tokens, routes, gates, ranking, counts, w_gate, w_up, w_down):
+    counts = counts.reshape(-1)
     own_rows, steps, width = tokens.shape
     planes = devices // 4
     block = own_rows * steps
@@ -241,15 +264,22 @@
     bf16, f32 = jnp.bfloat16, jnp.float32
     dma = pltpu.SemaphoreType.DMA
     in_vmem = pl.BlockSpec(memory_space=pltpu.VMEM)
-    in_smem = pl.BlockSpec(memory_space=pltpu.SMEM)
+    smem = pltpu.SMEM
     anywhere = pl.BlockSpec(memory_space=pl.ANY)
     return pl.pallas_call(
         functools.partial(kernel, planes),
         out_shape=jax.ShapeDtypeStruct(tokens.shape, bf16),
-        in_specs=[anywhere] + [in_smem] * 4 + [anywhere] * 3,
+        in_specs=[anywhere] * 8,
         out_specs=in_vmem,
         scratch_shapes=[
-            pltpu.VMEM((devices * own_rows, steps, width + LANES), bf16),
+            smem(routes.shape, routes.dtype),
+            smem(gates.shape, gates.dtype),
+            smem(ranking.shape, ranking.dtype),
+            smem(counts.shape, counts.dtype),
+            pltpu.VMEM(tokens.shape, bf16),
+            pltpu.VMEM((block, width + LANES), f32),
+            dma((4,)),
+            pltpu.VMEM((devices, block, width + LANES), bf16),
             pltpu.VMEM((4 * part, width + LANES), f32),
             pltpu.VMEM((4 * part, width), bf16),
             pltpu.VMEM((HOT, width, units), bf16),

time: 50.7 us -> 37.3 us (0.74)
  Pallas kernels: 47.7 us -> 35.6 us
  local copies, waits for them, and re-layouts: 2.75 us -> 1.45 us
    pallas_call x1, Pallas kernels: 47.7 us -> 35.6 us  [on_device(): pl.pallas_call(functools.partial(kernel, planes), out_shape=jax.ShapeDtyp...]
    unnamed x2 -> x1, local copies, waits for them, and re-layouts: 2.75 us -> 1.45 us
where the time goes in v2:
time: 37.3 us; the launch traced here: 37.1 us
  Pallas kernels  35.6 us (95%)
  local copies, waits for them, and re-layouts  1.45 us (4%)
    pallas_call x1, Pallas kernels, on_device(): pl.pallas_call(functools.partial(kernel, planes), out_shape=jax.ShapeDtyp...  35.6 us
    unnamed x1, local copies, waits for them, and re-layouts  1.45 us

profile of v2, /device:TPU:0, one launch (start us, length us, event | category | flops | bytes accessed | tf_op | source)
XLA Modules:
  0.0 37.1 jit_solution(11534763240555293823)
XLA Ops:
  0.0 35.6 %shard_map.82 = bf16[2,2,6144]{2,1,0:T(2,128)(2,1)} custom-call(bf16[2,2,6144]{2,1,0:T(2,128)(2,1)} %tokens.1, s32[2,2,2]{2,1,0:T(2,128)} %routes_hbm.1, f32[2,2,2]{2,1,0:T(2,128)} %gates_hbm.1, s32[8]{0:T(128)} %ranking_hbm.1, s32[2]{0:T(128)} %bitcast.1, bf16[2,6144,512]{2,1,0:T(8,128)(2,1)} %w_gate.1, bf16[2,6144,512]{2,1,0:T(8,128)(2,1)} %w_up.1, ...), custom_call_target="tpu_custom_call" | custom-call | tf_op jit(solution)/shard_map/pallas_call | solution.py:269
  35.6 1.5 %copy.10 = bf16[2,2,6144]{2,1,0:T(2,128)(2,1)} copy(bf16[2,2,6144]{2,1,0:T(2,128)(2,1)} %shard_map.82) | data formatting | bytes 98304

commit v3 on v2

--- a/solution.py
+++ b/solution.py
@@ -9,11 +9,11 @@
 
 HOT = 2
 LANES = 128
-K_PARTS = 4
-COL_PARTS = 6
-FIRST = 6
-STEP = 3
-LAG = 3
+K_PARTS = 2
+COL_PARTS = 4
+FIRST = 2
+STEP = 2
+LAG = 2
 MESH = pl.DeviceIdType.MESH
 
 

time: 37.3 us -> 36.1 us (0.968)
  Pallas kernels: 35.6 us -> 34.5 us
    pallas_call x1, Pallas kernels: 35.6 us -> 34.5 us  [on_device(): pl.pallas_call(functools.partial(kernel, planes), out_shape=jax.ShapeDtyp...]
where the time goes in v3:
time: 36.1 us; the launch traced here: 35.9 us
  Pallas kernels  34.5 us (96%)
  local copies, waits for them, and re-layouts  1.45 us (4%)
    pallas_call x1, Pallas kernels, on_device(): pl.pallas_call(functools.partial(kernel, planes), out_shape=jax.ShapeDtyp...  34.5 us
    unnamed x1, local copies, waits for them, and re-layouts  1.45 us

profile of v3, /device:TPU:0, one launch (start us, length us, event | category | flops | bytes accessed | tf_op | source)
XLA Modules:
  0.0 35.9 jit_solution(3430770232308749363)
XLA Ops:
  0.0 34.5 %shard_map.82 = bf16[2,2,6144]{2,1,0:T(2,128)(2,1)} custom-call(bf16[2,2,6144]{2,1,0:T(2,128)(2,1)} %tokens.1, s32[2,2,2]{2,1,0:T(2,128)} %routes_hbm.1, f32[2,2,2]{2,1,0:T(2,128)} %gates_hbm.1, s32[8]{0:T(128)} %ranking_hbm.1, s32[2]{0:T(128)} %bitcast.1, bf16[2,6144,512]{2,1,0:T(8,128)(2,1)} %w_gate.1, bf16[2,6144,512]{2,1,0:T(8,128)(2,1)} %w_up.1, ...), custom_call_target="tpu_custom_call" | custom-call | tf_op jit(solution)/shard_map/pallas_call | solution.py:269
  34.5 1.5 %copy.10 = bf16[2,2,6144]{2,1,0:T(2,128)(2,1)} copy(bf16[2,2,6144]{2,1,0:T(2,128)(2,1)} %shard_map.82) | data formatting | bytes 98304
